TPU v7x, 512 devices: a whole 4x4x16 slice. The times are simulated.
512 devices in a mesh: dp: 16 (over x, y), seq: 32 (over z, core).
Axes of the slice: x: 4, y: 4, z: 16, core: 2. Of those that a mesh axis runs over, the one named last changes fastest.
Arguments:
- queries: bfloat16 [16, 768, 2048], P('dp', 'seq'), may hold values from -18 to 18
- keys: bfloat16 [16, 8192, 2048], P('dp', 'seq'), may hold values from -18 to 18
- values: bfloat16 [16, 8192, 2048], P('dp', 'seq'), may hold values from -6 to 6
- attn_out: bfloat16 [16, 768, 2048], P('dp', 'seq'), may hold values from -3 to 3
- out_grad: bfloat16 [16, 768, 2048], P('dp', 'seq'), may hold values from -12 to 12
- loss_mask: int32 [16, 768], P('dp', 'seq'), may hold values from 0 to 1, as said below
- input_lengths: int32 [16, 1, 4], P('dp'), may hold values from 1 to 4096, 8192 in all within a row
- target_lengths: int32 [16, 1, 4], P('dp'), may hold values from 1 to 384, 768 in all within a row
Outputs:
- grad_queries: bfloat16 [16, 768, 2048], P('dp', 'seq')
- grad_keys: bfloat16 [16, 8192, 2048], P('dp', 'seq')
- grad_values: bfloat16 [16, 8192, 2048], P('dp', 'seq')
Inputs may be any that keep to these rules, and one draw needn't show every extreme that they name: `loss_mask`: the first of each device's 24 target rows carries loss.
All inputs are finite; a program needn't handle non-finite values.
Results may differ from a plain program's by a relative error of at most 0.0095.
Values may be sent and summed in bfloat16 or wider, within the bound.
A program may use at most 128 MiB of HBM per device.

v0:
```python
import jax
import jax.numpy as jnp
from jax import lax
from jax.sharding import PartitionSpec as P

HEADS = 8
HEAD_SIZE = 256


def swapped(block, axis, apart):
    count = lax.axis_size(axis)
    route = []
    for low in range(count):
        high = low | 1 << apart
        if high != low and high < count:
            route += [(low, high), (high, low)]
    return lax.ppermute(block, axis, route)


def for_sending(shard):
    return jax.tree.map(lambda a: a.astype(jnp.bfloat16) if a.dtype == jnp.float32 else a, shard)


def document_ids(lengths, positions):
    doc_ends = jnp.cumsum(lengths)
    return jnp.sum((positions[:, None] >= doc_ends[None, :]).astype(jnp.int32), axis=1)


def score_block(query_rows, key_rows):
    query_heads = query_rows.reshape(query_rows.shape[0], HEADS, HEAD_SIZE)
    key_heads = key_rows.reshape(key_rows.shape[0], HEADS, HEAD_SIZE)
    return jnp.einsum(
        "rhd,ehd->hre", query_heads, key_heads, preferred_element_type=jnp.float32
    ) * HEAD_SIZE ** (-0.5)


def partial_stats(scores, allowed):
    masked_scores = jnp.where(allowed[None], scores, -1e30)
    row_top = jnp.max(masked_scores, axis=2)
    row_total = jnp.sum(
        jnp.where(allowed[None], jnp.exp(scores - row_top[:, :, None]), 0.0), axis=2
    )
    return (row_top, row_total)


def combine_stats(row_top, row_total, bit_count):
    for bit_number in range(bit_count):
        other_top, other_total = swapped((row_top, row_total), "seq", bit_number)
        new_top = jnp.maximum(row_top, other_top)
        row_total = row_total * jnp.exp(row_top - new_top) + other_total * jnp.exp(
            other_top - new_top
        )
        row_top = new_top
    return row_top + jnp.log(row_total)


def tile_grads(scores, allowed, log_total, query_rows, grad_rows, delta_rows, key_rows, value_rows):
    dec_count = query_rows.shape[0]
    enc_count = key_rows.shape[0]
    inverse_root = HEAD_SIZE ** (-0.5)
    query_heads = query_rows.reshape(dec_count, HEADS, HEAD_SIZE)
    grad_heads = grad_rows.reshape(dec_count, HEADS, HEAD_SIZE)
    key_heads = key_rows.reshape(enc_count, HEADS, HEAD_SIZE)
    value_heads = value_rows.reshape(enc_count, HEADS, HEAD_SIZE)
    probs = jnp.where(allowed[None], jnp.exp(scores - log_total[:, :, None]), 0.0)
    dprob = jnp.einsum("rhd,ehd->hre", grad_heads, value_heads, preferred_element_type=jnp.float32)
    dscore = probs * (dprob - delta_rows.astype(jnp.float32).T[:, :, None])
    probs_low = probs.astype(jnp.bfloat16)
    dscore_low = dscore.astype(jnp.bfloat16)
    dvalue = jnp.einsum(
        "hre,rhd->ehd", probs_low, grad_heads, preferred_element_type=jnp.float32
    ).reshape(enc_count, HEADS * HEAD_SIZE)
    dkey = (
        jnp.einsum(
            "hre,rhd->ehd", dscore_low, query_heads, preferred_element_type=jnp.float32
        ).reshape(enc_count, HEADS * HEAD_SIZE)
        * inverse_root
    )
    dquery = (
        jnp.einsum(
            "hre,ehd->rhd", dscore_low, key_heads, preferred_element_type=jnp.float32
        ).reshape(dec_count, HEADS * HEAD_SIZE)
        * inverse_root
    )
    return (dquery, dkey, dvalue)


def local(queries, keys, values, attn_out, out_grad, loss_mask, input_lengths, target_lengths):
    query_rows = queries[0]
    key_rows = keys[0]
    value_rows = values[0]
    dec_local = query_rows.shape[0]
    enc_local = key_rows.shape[0]
    seq_count = lax.axis_size("seq")
    bit_count = seq_count.bit_length() - 1
    local_index = lax.axis_index("seq")
    group_rows = seq_count * dec_local
    mask_rows = loss_mask[0]
    count = lax.psum(jnp.sum(mask_rows).astype(jnp.float32), ("dp", "seq"))
    factor = jnp.float32(dec_local * lax.axis_size("dp") * seq_count) / count
    masked = out_grad[0] * mask_rows[:, None].astype(jnp.bfloat16)
    delta = jnp.sum(
        (masked.astype(jnp.float32) * attn_out[0].astype(jnp.float32)).reshape(
            dec_local, HEADS, HEAD_SIZE
        ),
        axis=2,
    ).astype(jnp.bfloat16)
    collected = (query_rows, masked, delta)
    for bit_number in range(bit_count):
        partner = jax.tree.map(
            lambda part, own: part.astype(own.dtype),
            swapped(for_sending(collected), "seq", bit_number),
            collected,
        )
        upper = local_index >> bit_number & 1 == 1
        collected = tuple(
            (
                jnp.where(
                    upper,
                    jnp.concatenate([theirs, own_part], 0),
                    jnp.concatenate([own_part, theirs], 0),
                )
                for own_part, theirs in zip(collected, partner)
            )
        )
    block_query, block_grad, block_delta = collected
    input_lens = input_lengths[0, 0]
    target_lens = target_lengths[0, 0]
    enc_doc = document_ids(
        input_lens, local_index * enc_local + jnp.arange(enc_local, dtype=jnp.int32)
    )
    dec_doc = document_ids(target_lens, jnp.arange(group_rows, dtype=jnp.int32))
    allowed = dec_doc[:, None] == enc_doc[None, :]
    scores = score_block(block_query, key_rows)
    row_top, row_total = partial_stats(scores, allowed)
    log_total = combine_stats(row_top, row_total, bit_count)
    dquery, dkey, dvalue = tile_grads(
        scores, allowed, log_total, block_query, block_grad, block_delta, key_rows, value_rows
    )
    summed = dquery
    for bit_number in reversed(range(bit_count)):
        half_rows = summed.shape[0] // 2
        lower_half = summed[:half_rows]
        upper_half = summed[half_rows:]
        upper = local_index >> bit_number & 1 == 1
        outgoing = jnp.where(upper, lower_half, upper_half)
        kept = jnp.where(upper, upper_half, lower_half)
        summed = kept + swapped(outgoing, "seq", bit_number)
    grad_queries = (factor * summed).astype(jnp.bfloat16)[None]
    grad_keys = (factor * dkey).astype(jnp.bfloat16)[None]
    grad_values = (factor * dvalue).astype(jnp.bfloat16)[None]
    return (grad_queries, grad_keys, grad_values)


def solution(mesh):
    return jax.shard_map(
        local,
        mesh=mesh,
        in_specs=(
            P("dp", "seq", None),
            P("dp", "seq", None),
            P("dp", "seq", None),
            P("dp", "seq", None),
            P("dp", "seq", None),
            P("dp", "seq"),
            P("dp", None, None),
            P("dp", None, None),
        ),
        out_specs=(P("dp", "seq", None), P("dp", "seq", None), P("dp", "seq", None)),
        check_vma=False,
    )
```

profile of v0, /device:TPU:1, one launch (start us, length us, event | category | flops | bytes accessed | tf_op | source)
XLA Modules:
  0.0 1133.4 jit_solution(13357704482957189738)
XLA Ops:
  0.7 8.9 collective-permute-start
  15.0 4.8 collective-permute-done.1
  27.7 14.4 %collective-permute-done.2 = bf16[96,2048]{1,0:T(8,128)(2,1)S(1)} collective-permute-done((bf16[96,2048]{1,0:T(8,128)(2,1)S(1)}, bf16[96,2048]{1,0:T(8,128)(2,1)S(1)}, u32[]{:S(2)}, u32[]{:S(2)}) %collective-permute-start.2) | collective-permute-done | bytes 393248 | tf_op jit(solution)/shard_map/ppermute | solution.py:17
  43.0 3.5 collective-permute-start.3
  53.3 12.9 %collective-permute-done.16 = bf16[48,2048]{1,0:T(8,128)(2,1)S(1)} collective-permute-done((bf16[48,2048]{1,0:T(8,128)(2,1)S(1)}, bf16[48,2048]{1,0:T(8,128)(2,1)S(1)}, u32[]{:S(2)}, u32[]{:S(2)}) %collective-permute-start.16) | collective-permute-done | bytes 196640 | tf_op jit(solution)/shard_map/ppermute | solution.py:17
  67.0 34.7 %collective-permute-start.17 = (bf16[96,2048]{1,0:T(8,128)(2,1)S(1)}, bf16[96,2048]{1,0:T(8,128)(2,1)S(1)}, u32[]{:S(2)}, u32[]{:S(2)}) collective-permute-start(bf16[96,2048]{1,0:T(8,128)(2,1)S(1)} %maximum_select_fusion.17), channel_id=1, source_target_pairs={{0,4},{4,0},{1,5},{5,1},{2,6},{6,2},{3,7},{7,3},{8,12},{12,8},{9,1... | collective-permute-start | bytes 1179656 | tf_op jit(solution)/shard_map/ppermute | solution.py:17
  102.0 14.3 %collective-permute-done.3 = bf16[192,2048]{1,0:T(8,128)(2,1)S(1)} collective-permute-done((bf16[192,2048]{1,0:T(8,128)(2,1)S(1)}, bf16[192,2048]{1,0:T(8,128)(2,1)S(1)}, u32[]{:S(2)}, u32[]{:S(2)}) %collective-permute-start.3) | collective-permute-done | bytes 786464 | tf_op jit(solution)/shard_map/ppermute | solution.py:17
  118.1 73.9 %collective-permute-start.4 = (bf16[384,2048]{1,0:T(8,128)(2,1)}, bf16[384,2048]{1,0:T(8,128)(2,1)}, u32[]{:S(2)}, u32[]{:S(2)}) collective-permute-start(bf16[384,2048]{1,0:T(8,128)(2,1)} %maximum_select_fusion.2), channel_id=1, source_target_pairs={{0,16},{16,0},{1,17},{17,1},{2,18},{18,2},{3,19},{19,3},{4,20},{20... | collective-permute-start | bytes 4718600 | tf_op jit(solution)/shard_map/ppermute | solution.py:17
  194.0 74.2 %collective-permute-done.17 = bf16[96,2048]{1,0:T(8,128)(2,1)S(1)} collective-permute-done((bf16[96,2048]{1,0:T(8,128)(2,1)S(1)}, bf16[96,2048]{1,0:T(8,128)(2,1)S(1)}, u32[]{:S(2)}, u32[]{:S(2)}) %collective-permute-start.17) | collective-permute-done | bytes 393248 | tf_op jit(solution)/shard_map/ppermute | solution.py:17
  278.9 10.2 collective-permute-done.22
  289.2 24.3 %collective-permute-start.23 = (bf16[192,8]{0,1:T(8,128)(2,1)S(1)}, bf16[192,8]{0,1:T(8,128)(2,1)S(1)}, u32[]{:S(2)}, u32[]{:S(2)}) collective-permute-start(bf16[192,8]{0,1:T(8,128)(2,1)S(1)} %maximum_select_fusion.22), channel_id=1, source_target_pairs={{0,8},{8,0},{1,9},{9,1},{2,10},{10,2},{3,11},{11,3},{4,12},{12,4},... | collective-permute-start | bytes 9224 | tf_op jit(solution)/shard_map/ppermute | solution.py:17
  318.8 57.9 %collective-permute-done.18 = bf16[192,2048]{1,0:T(8,128)(2,1)S(1)} collective-permute-done((bf16[192,2048]{1,0:T(8,128)(2,1)}, bf16[192,2048]{1,0:T(8,128)(2,1)S(1)}, u32[]{:S(2)}, u32[]{:S(2)}) %collective-permute-start.18) | collective-permute-done | bytes 786464 | tf_op jit(solution)/shard_map/ppermute | solution.py:17
  380.1 9.8 collective-permute-start.19
  395.6 4.2 select_reduce_fusion.1
  406.1 4.2 collective-permute-start.24
  415.6 35.0 %collective-permute-done.24 = bf16[384,8]{0,1:T(8,128)(2,1)S(1)} collective-permute-done((bf16[384,8]{0,1:T(8,128)(2,1)S(1)}, bf16[384,8]{0,1:T(8,128)(2,1)S(1)}, u32[]{:S(2)}, u32[]{:S(2)}) %collective-permute-start.24) | collective-permute-done | bytes 6176 | tf_op jit(solution)/shard_map/ppermute | solution.py:17
  451.8 31.5 %collective-permute-done.6 = f32[8,768]{1,0:T(8,128)S(1)} collective-permute-done((f32[8,768]{1,0:T(8,128)S(1)}, f32[8,768]{1,0:T(8,128)S(1)}, u32[]{:S(2)}, u32[]{:S(2)}) %collective-permute-start.6) | collective-permute-done | bytes 24608 | tf_op jit(solution)/shard_map/ppermute | solution.py:17
  483.9 5.4 collective-permute-start.12
  495.9 5.0 collective-permute-start.13
  500.9 4.2 collective-permute-start.8
  509.4 11.7 %collective-permute-start.14 = (f32[8,768]{1,0:T(8,128)S(1)}, f32[8,768]{1,0:T(8,128)S(1)}, u32[]{:S(2)}, u32[]{:S(2)}) collective-permute-start(f32[8,768]{1,0:T(8,128)S(1)} %get-tuple-element.18), channel_id=1, source_target_pairs={{0,16},{16,0},{1,17},{17,1},{2,18},{18,2},{3,19},{19,3},{4,20},{20... | collective-permute-start | bytes 73736 | tf_op jit(solution)/shard_map/ppermute | solution.py:17
  527.7 6.9 collective-permute-done.9
  534.6 6.9 multiply_convert_fusion
  545.6 3.5 copy.180
  549.1 5.3 collective-permute-start.25
  556.8 208.6 %collective-permute-done.25 = f32[384,2048]{1,0:T(8,128)} collective-permute-done((f32[384,2048]{1,0:T(8,128)}, f32[384,2048]{1,0:T(8,128)}, u32[]{:S(2)}, u32[]{:S(2)}) %collective-permute-start.25) | collective-permute-done | bytes 3145760 | tf_op jit(solution)/shard_map/ppermute | solution.py:17
  765.4 3.5 add.53
  771.0 191.7 %collective-permute-done.26 = f32[192,2048]{1,0:T(8,128)S(1)} collective-permute-done((f32[192,2048]{1,0:T(8,128)S(1)}, f32[192,2048]{1,0:T(8,128)S(1)}, u32[]{:S(2)}, u32[]{:S(2)}) %collective-permute-start.26) | collective-permute-done | bytes 1572896 | tf_op jit(solution)/shard_map/ppermute | solution.py:17
  966.5 143.7 %psum.7 = f32[]{:T(128)} all-reduce(f32[]{:T(128)S(6)} %convert_element_type.84), channel_id=1, replica_groups=mesh['dp'=16,'seq'=32] {'dp','seq'}, use_global_device_ids=true, to_apply=%region_1.0 | all-reduce | flops 1 | bytes 8 | tf_op jit(solution)/shard_map/psum | solution.py:99
  1112.4 4.1 collective-permute-start.28
  1116.5 4.9 multiply_convert_fusion.1
  1121.4 3.7 collective-permute-done.28
  (143 shorter events, 103.0 us)
Async XLA Ops:
  0.7 10.1 collective-permute-start
  11.7 8.0 collective-permute-start.1
  19.8 22.2 %collective-permute-start.2 = (bf16[96,2048]{1,0:T(8,128)(2,1)S(1)}, bf16[96,2048]{1,0:T(8,128)(2,1)S(1)}, u32[]{:S(2)}, u32[]{:S(2)}) collective-permute-start(bf16[96,2048]{1,0:T(8,128)(2,1)S(1)} %maximum_select_fusion.16), channel_id=1, source_target_pairs={{0,4},{4,0},{1,5},{5,1},{2,6},{6,2},{3,7},{7,3},{8,12},{12,8},{9,1... | collective-permute-start | bytes 1179656 | tf_op jit(solution)/shard_map/ppermute | solution.py:17
  22.7 23.8 %collective-permute-start.15 = (bf16[24,2048]{1,0:T(8,128)(2,1)S(1)}, bf16[24,2048]{1,0:T(8,128)(2,1)S(1)}, u32[]{:S(2)}, u32[]{:S(2)}) collective-permute-start(bf16[24,2048]{1,0:T(8,128)(2,1)S(1)} %bitcast_multiply_fusion), channel_id=1, source_target_pairs={{0,1},{1,0},{2,3},{3,2},{4,5},{5,4},{6,7},{7,6},{8,9},{9,8},{10,11... | collective-permute-start | bytes 294920 | tf_op jit(solution)/shard_map/ppermute | solution.py:17
  43.0 73.3 %collective-permute-start.3 = (bf16[192,2048]{1,0:T(8,128)(2,1)S(1)}, bf16[192,2048]{1,0:T(8,128)(2,1)S(1)}, u32[]{:S(2)}, u32[]{:S(2)}) collective-permute-start(bf16[192,2048]{1,0:T(8,128)(2,1)S(1)} %maximum_select_fusion.8), channel_id=1, source_target_pairs={{0,8},{8,0},{1,9},{9,1},{2,10},{10,2},{3,11},{11,3},{4,12},{12,4},... | collective-permute-start | bytes 2359304 | tf_op jit(solution)/shard_map/ppermute | solution.py:17
  46.6 229.8 %copy-start.5 = (bf16[48,2048]{1,0:T(8,128)(2,1)}, bf16[48,2048]{1,0:T(8,128)(2,1)S(1)}, u32[]{:S(2)}) copy-start(bf16[48,2048]{1,0:T(8,128)(2,1)S(1)} %maximum_select_fusion.19) | copy-start | bytes 589828
  46.6 19.7 %collective-permute-start.16 = (bf16[48,2048]{1,0:T(8,128)(2,1)S(1)}, bf16[48,2048]{1,0:T(8,128)(2,1)S(1)}, u32[]{:S(2)}, u32[]{:S(2)}) collective-permute-start(bf16[48,2048]{1,0:T(8,128)(2,1)S(1)} %maximum_select_fusion.19), channel_id=1, source_target_pairs={{0,2},{2,0},{1,3},{3,1},{4,6},{6,4},{5,7},{7,5},{8,10},{10,8},{9,1... | collective-permute-start | bytes 589832 | tf_op jit(solution)/shard_map/ppermute | solution.py:17
  50.2 141.8 %collective-permute-start.20 = (bf16[24,8]{0,1:T(8,128)(2,1)S(1)}, bf16[24,8]{0,1:T(8,128)(2,1)S(1)}, u32[]{:S(2)}, u32[]{:S(2)}) collective-permute-start(bf16[24,8]{0,1:T(8,128)(2,1)S(1)} %copy.176), channel_id=1, source_target_pairs={{0,1},{1,0},{2,3},{3,2},{4,5},{5,4},{6,7},{7,6},{8,9},{9,8},{10,11... | collective-permute-start | bytes 1160 | tf_op jit(solution)/shard_map/ppermute | solution.py:17
  67.0 201.2 %collective-permute-start.17 = (bf16[96,2048]{1,0:T(8,128)(2,1)S(1)}, bf16[96,2048]{1,0:T(8,128)(2,1)S(1)}, u32[]{:S(2)}, u32[]{:S(2)}) collective-permute-start(bf16[96,2048]{1,0:T(8,128)(2,1)S(1)} %maximum_select_fusion.17), channel_id=1, source_target_pairs={{0,4},{4,0},{1,5},{5,1},{2,6},{6,2},{3,7},{7,3},{8,12},{12,8},{9,1... | collective-permute-start | bytes 1179656 | tf_op jit(solution)/shard_map/ppermute | solution.py:17
  116.3 158.6 %copy-start.4 = (bf16[192,2048]{1,0:T(8,128)(2,1)}, bf16[192,2048]{1,0:T(8,128)(2,1)S(1)}, u32[]{:S(2)}) copy-start(bf16[192,2048]{1,0:T(8,128)(2,1)S(1)} %collective-permute-done.3) | copy-start | bytes 2359300
  118.1 275.6 %collective-permute-start.4 = (bf16[384,2048]{1,0:T(8,128)(2,1)}, bf16[384,2048]{1,0:T(8,128)(2,1)}, u32[]{:S(2)}, u32[]{:S(2)}) collective-permute-start(bf16[384,2048]{1,0:T(8,128)(2,1)} %maximum_select_fusion.2), channel_id=1, source_target_pairs={{0,16},{16,0},{1,17},{17,1},{2,18},{18,2},{3,19},{19,3},{4,20},{20... | collective-permute-start | bytes 4718600 | tf_op jit(solution)/shard_map/ppermute | solution.py:17
  192.0 80.0 %collective-permute-start.21 = (bf16[48,8]{0,1:T(8,128)(2,1)S(1)}, bf16[48,8]{0,1:T(8,128)(2,1)S(1)}, u32[]{:S(2)}, u32[]{:S(2)}) collective-permute-start(bf16[48,8]{0,1:T(8,128)(2,1)S(1)} %maximum_select_fusion.23), channel_id=1, source_target_pairs={{0,2},{2,0},{1,3},{3,1},{4,6},{6,4},{5,7},{7,5},{8,10},{10,8},{9,1... | collective-permute-start | bytes 2312 | tf_op jit(solution)/shard_map/ppermute | solution.py:17
  270.0 106.7 %collective-permute-start.18 = (bf16[192,2048]{1,0:T(8,128)(2,1)}, bf16[192,2048]{1,0:T(8,128)(2,1)S(1)}, u32[]{:S(2)}, u32[]{:S(2)}) collective-permute-start(bf16[192,2048]{1,0:T(8,128)(2,1)} %maximum_select_fusion.9), channel_id=1, source_target_pairs={{0,8},{8,0},{1,9},{9,1},{2,10},{10,2},{3,11},{11,3},{4,12},{12,4},... | collective-permute-start | bytes 2359304 | tf_op jit(solution)/shard_map/ppermute | solution.py:17
  272.1 17.0 %collective-permute-start.22 = (bf16[96,8]{0,1:T(8,128)(2,1)S(1)}, bf16[96,8]{0,1:T(8,128)(2,1)S(1)}, u32[]{:S(2)}, u32[]{:S(2)}) collective-permute-start(bf16[96,8]{0,1:T(8,128)(2,1)S(1)} %maximum_select_fusion.24), channel_id=1, source_target_pairs={{0,4},{4,0},{1,5},{5,1},{2,6},{6,2},{3,7},{7,3},{8,12},{12,8},{9,1... | collective-permute-start | bytes 4616 | tf_op jit(solution)/shard_map/ppermute | solution.py:17
  289.2 116.8 %collective-permute-start.23 = (bf16[192,8]{0,1:T(8,128)(2,1)S(1)}, bf16[192,8]{0,1:T(8,128)(2,1)S(1)}, u32[]{:S(2)}, u32[]{:S(2)}) collective-permute-start(bf16[192,8]{0,1:T(8,128)(2,1)S(1)} %maximum_select_fusion.22), channel_id=1, source_target_pairs={{0,8},{8,0},{1,9},{9,1},{2,10},{10,2},{3,11},{11,3},{4,12},{12,4},... | collective-permute-start | bytes 9224 | tf_op jit(solution)/shard_map/ppermute | solution.py:17
  380.1 145.7 %collective-permute-start.19 = (bf16[384,2048]{1,0:T(8,128)(2,1)}, bf16[384,2048]{1,0:T(8,128)(2,1)}, u32[]{:S(2)}, u32[]{:S(2)}) collective-permute-start(bf16[384,2048]{1,0:T(8,128)(2,1)} %maximum_select_fusion.4), channel_id=1, source_target_pairs={{0,16},{16,0},{1,17},{17,1},{2,18},{18,2},{3,19},{19,3},{4,20},{20... | collective-permute-start | bytes 4718600 | tf_op jit(solution)/shard_map/ppermute | solution.py:17
  399.8 10.5 collective-permute-start.5
  403.9 6.4 collective-permute-start.10
  406.1 44.5 %collective-permute-start.24 = (bf16[384,8]{0,1:T(8,128)(2,1)S(1)}, bf16[384,8]{0,1:T(8,128)(2,1)S(1)}, u32[]{:S(2)}, u32[]{:S(2)}) collective-permute-start(bf16[384,8]{0,1:T(8,128)(2,1)S(1)} %maximum_select_fusion.21), channel_id=1, source_target_pairs={{0,16},{16,0},{1,17},{17,1},{2,18},{18,2},{3,19},{19,3},{4,20},{20... | collective-permute-start | bytes 18440 | tf_op jit(solution)/shard_map/ppermute | solution.py:17
  410.3 41.4 %collective-permute-start.11 = (f32[8,768]{1,0:T(8,128)S(1)}, f32[8,768]{1,0:T(8,128)S(1)}, u32[]{:S(2)}, u32[]{:S(2)}) collective-permute-start(f32[8,768]{1,0:T(8,128)S(1)} %get-tuple-element.24), channel_id=1, source_target_pairs={{0,2},{2,0},{1,3},{3,1},{4,6},{6,4},{5,7},{7,5},{8,10},{10,8},{9,1... | collective-permute-start | bytes 73736 | tf_op jit(solution)/shard_map/ppermute | solution.py:17
  412.3 71.0 %collective-permute-start.6 = (f32[8,768]{1,0:T(8,128)S(1)}, f32[8,768]{1,0:T(8,128)S(1)}, u32[]{:S(2)}, u32[]{:S(2)}) collective-permute-start(f32[8,768]{1,0:T(8,128)S(1)} %get-tuple-element.25), channel_id=1, source_target_pairs={{0,2},{2,0},{1,3},{3,1},{4,6},{6,4},{5,7},{7,5},{8,10},{10,8},{9,1... | collective-permute-start | bytes 73736 | tf_op jit(solution)/shard_map/ppermute | solution.py:17
  483.9 8.4 collective-permute-start.12
  489.3 5.8 collective-permute-start.7
  495.9 11.5 %collective-permute-start.13 = (f32[8,768]{1,0:T(8,128)S(1)}, f32[8,768]{1,0:T(8,128)S(1)}, u32[]{:S(2)}, u32[]{:S(2)}) collective-permute-start(f32[8,768]{1,0:T(8,128)S(1)} %get-tuple-element.20), channel_id=1, source_target_pairs={{0,8},{8,0},{1,9},{9,1},{2,10},{10,2},{3,11},{11,3},{4,12},{12,4},... | collective-permute-start | bytes 73736 | tf_op jit(solution)/shard_map/ppermute | solution.py:17
  500.9 8.5 collective-permute-start.8
  509.4 18.3 %collective-permute-start.14 = (f32[8,768]{1,0:T(8,128)S(1)}, f32[8,768]{1,0:T(8,128)S(1)}, u32[]{:S(2)}, u32[]{:S(2)}) collective-permute-start(f32[8,768]{1,0:T(8,128)S(1)} %get-tuple-element.18), channel_id=1, source_target_pairs={{0,16},{16,0},{1,17},{17,1},{2,18},{18,2},{3,19},{19,3},{4,20},{20... | collective-permute-start | bytes 73736 | tf_op jit(solution)/shard_map/ppermute | solution.py:17
  521.1 13.4 %collective-permute-start.9 = (f32[8,768]{1,0:T(8,128)S(1)}, f32[8,768]{1,0:T(8,128)S(1)}, u32[]{:S(2)}, u32[]{:S(2)}) collective-permute-start(f32[8,768]{1,0:T(8,128)S(1)} %get-tuple-element.19), channel_id=1, source_target_pairs={{0,16},{16,0},{1,17},{17,1},{2,18},{18,2},{3,19},{19,3},{4,20},{20... | collective-permute-start | bytes 73736 | tf_op jit(solution)/shard_map/ppermute | solution.py:17
  549.1 216.3 %collective-permute-start.25 = (f32[384,2048]{1,0:T(8,128)}, f32[384,2048]{1,0:T(8,128)}, u32[]{:S(2)}, u32[]{:S(2)}) collective-permute-start(f32[384,2048]{1,0:T(8,128)} %copy.180), channel_id=1, source_target_pairs={{0,16},{16,0},{1,17},{17,1},{2,18},{18,2},{3,19},{19,3},{4,20},{20... | collective-permute-start | bytes 9437192 | tf_op jit(solution)/shard_map/ppermute | solution.py:17
  769.1 193.6 %collective-permute-start.26 = (f32[192,2048]{1,0:T(8,128)S(1)}, f32[192,2048]{1,0:T(8,128)S(1)}, u32[]{:S(2)}, u32[]{:S(2)}) collective-permute-start(f32[192,2048]{1,0:T(8,128)S(1)} %slice_select_fusion.2), channel_id=1, source_target_pairs={{0,8},{8,0},{1,9},{9,1},{2,10},{10,2},{3,11},{11,3},{4,12},{12,4},... | collective-permute-start | bytes 4718600 | tf_op jit(solution)/shard_map/ppermute | solution.py:17
  964.0 146.9 %collective-permute-start.27 = (f32[96,2048]{1,0:T(8,128)}, f32[96,2048]{1,0:T(8,128)}, u32[]{:S(2)}, u32[]{:S(2)}) collective-permute-start(f32[96,2048]{1,0:T(8,128)} %slice_select_fusion.3), channel_id=1, source_target_pairs={{0,4},{4,0},{1,5},{5,1},{2,6},{6,2},{3,7},{7,3},{8,12},{12,8},{9,1... | collective-permute-start | bytes 2359304 | tf_op jit(solution)/shard_map/ppermute | solution.py:17
  1112.4 12.7 %collective-permute-start.28 = (f32[48,2048]{1,0:T(8,128)S(1)}, f32[48,2048]{1,0:T(8,128)S(1)}, u32[]{:S(2)}, u32[]{:S(2)}) collective-permute-start(f32[48,2048]{1,0:T(8,128)S(1)} %slice_select_fusion.4), channel_id=1, source_target_pairs={{0,2},{2,0},{1,3},{3,1},{4,6},{6,4},{5,7},{7,5},{8,10},{10,8},{9,1... | collective-permute-start | bytes 1179656 | tf_op jit(solution)/shard_map/ppermute | solution.py:17
  1125.2 7.6 collective-permute-start.29
  (21 other events, 603.2 us)
where the time goes:
time: 1130 us
  waiting for transfers between devices  672 us (59%)
  starting transfers between devices  236 us (21%)
  blocking collectives  144 us (13%)
  other arithmetic  34.4 us (3%)
  local copies, waits for them, and re-layouts  26.9 us (2%)
  matrix products  18.3 us (2%)
    ppermute x30, waiting for transfers between devices, swapped(): return lax.ppermute(block, axis, route)  672 us
    ppermute x30, starting transfers between devices, swapped(): return lax.ppermute(block, axis, route)  236 us
    psum x1, blocking collectives, local(): count = lax.psum(jnp.sum(mask_rows).astype(jnp.float32), ('dp', 'seq'))  144 us
  transfers between devices with their start and end apart: 30, of which 16 were waited for; matrix products, arithmetic and copies ran while one was open for 5% of the time, Pallas kernels for 0%

commit v1 on v0

v1 whole, which is shorter than its diff:
```python
import functools

import jax
import jax.numpy as jnp
from jax import lax
from jax.experimental import pallas as pl
from jax.experimental.pallas import tpu as pltpu
from jax.sharding import PartitionSpec as P

HEADS = 8
HEAD_SIZE = 256
HALF_HEADS = HEADS // 2
HALF = HALF_HEADS * HEAD_SIZE
LANES = 128
CHUNKS = 2
LAG = 4
NEVER = -1e30
MESH = pl.DeviceIdType.MESH


def nt(a, b):
    return lax.dot_general(a, b, (((1,), (1,)), ((), ())), preferred_element_type=jnp.float32)


def tn(a, b):
    return lax.dot_general(a, b, (((0,), (0,)), ((), ())), preferred_element_type=jnp.float32)


def nn(a, b):
    return jnp.dot(a, b, preferred_element_type=jnp.float32)


def kernel(
    dp_x,
    dp_y,
    chips,
    in_len,
    out_len,
    q_ref,
    g_ref,
    a_ref,
    mask_ref,
    k_ref,
    v_ref,
    dq_ref,
    dk_ref,
    dv_ref,
    stage_out,
    stage_in,
    kx,
    vx,
    qb,
    mb,
    kdoc,
    scores,
    probs,
    dscores,
    dq_part,
    rs_in,
    rs_out,
    grads,
    fin,
    fin_in,
    tile_out,
    tile_in,
    log_out,
    log_in,
    row_info,
    count_out,
    count_in,
    kv_local,
    kv_send,
    kv_recv,
    stage_send,
    stage_recv,
    ag_send,
    ag_recv,
    rs_send,
    rs_recv,
    tile_send,
    tile_recv,
    log_send,
    log_recv,
    count_send,
    count_recv,
    out_local,
    out_send,
    out_recv,
    fin_send,
    fin_recv,
):
    rows = q_ref.shape[0]
    keys_dev = k_ref.shape[0]
    block = 2 * rows
    keys_chip = 2 * keys_dev
    slots = chips // 2
    wide = HALF // CHUNKS
    dp = lax.axis_index("dp")
    seq = lax.axis_index("seq")
    z = seq // 2
    core = seq % 2
    sibling = (dp, z * 2 + 1 - core)

    def chip_at(offset):
        return (dp, ((z + offset + chips) % chips) * 2 + core)

    ahead = (chip_at(1), chip_at(-1))
    peers_x = [((dp + dp_y * k) % (dp_x * dp_y), seq) for k in range(1, dp_x)]
    peers_y = [((dp // dp_y) * dp_y + (dp % dp_y + k) % dp_y, seq) for k in range(1, dp_y)]

    mine = pl.ds(pl.multiple_of(core * HALF, HALF), HALF)
    theirs = pl.ds(pl.multiple_of((1 - core) * HALF, HALF), HALF)
    my_keys = pl.ds(pl.multiple_of(core * keys_dev, keys_dev), keys_dev)
    their_keys = pl.ds(pl.multiple_of((1 - core) * keys_dev, keys_dev), keys_dev)

    def remote(src, dst, send, recv, device):
        return pltpu.make_async_remote_copy(
            src_ref=src, dst_ref=dst, send_sem=send, recv_sem=recv, device_id=device, device_id_type=MESH
        )

    kv_own = [
        pltpu.make_async_copy(ref.at[:, mine], buf.at[my_keys], kv_local.at[i])
        for i, (ref, buf) in enumerate(((k_ref, kx), (v_ref, vx)))
    ]
    kv_sent = [
        remote(ref.at[:, theirs], buf.at[my_keys], kv_send.at[i], kv_recv.at[i], sibling)
        for i, (ref, buf) in enumerate(((k_ref, kx), (v_ref, vx)))
    ]
    staged = [
        remote(stage_out.at[i], stage_in.at[i], stage_send.at[i], stage_recv.at[i], sibling) for i in range(3)
    ]
    count_swap = remote(count_out.at[2], count_in.at[2, 0], stage_send.at[3], stage_recv.at[3], sibling)

    def gathered(which, way, hop, chunk):
        buf = (qb, mb)[which]
        source = hop * LANES + (way * block if hop else 0)
        target = block if hop == slots - 1 else (hop + 1) * LANES + way * block
        columns = pl.ds(chunk * wide, wide)
        return remote(
            buf.at[pl.ds(source, block), columns],
            buf.at[pl.ds(target, block), columns],
            ag_send.at[which, way, hop, chunk],
            ag_recv.at[which, way, hop, chunk],
            ahead[way],
        )

    def chunks_of_hop(way, hop, last):
        if hop != last:
            return range(CHUNKS)
        return range(CHUNKS // 2) if way == 0 else range(CHUNKS // 2, CHUNKS)

    def forward(which, hop):
        for chunk in range(CHUNKS):
            for way in range(2):
                if chunk in chunks_of_hop(way, hop, slots - 1):
                    gathered(which, way, hop, chunk).wait_recv()
                    if hop + 1 < slots and chunk in chunks_of_hop(way, hop + 1, slots - 1):
                        gathered(which, way, hop + 1, chunk).start()

    def scattered(way, hop, chunk):
        columns = pl.ds(chunk * wide, wide)
        return remote(
            rs_out.at[way, hop, :, columns],
            rs_in.at[way, hop, :, columns],
            rs_send.at[way, hop, chunk],
            rs_recv.at[way, hop, chunk],
            ahead[way],
        )

    def tile_copies(slot):
        if slot == 0:
            return [remote(tile_out.at[0], tile_in.at[slots], tile_send.at[slots], tile_recv.at[slots], chip_at(slots))]
        return [
            remote(tile_out.at[slot], tile_in.at[slot], tile_send.at[slot], tile_recv.at[slot], chip_at(-slot)),
            remote(
                tile_out.at[slot],
                tile_in.at[slots + slot],
                tile_send.at[slots + slot],
                tile_recv.at[slots + slot],
                chip_at(slot),
            ),
        ]

    def log_copy(offset):
        return remote(log_out, log_in.at[offset], log_send.at[offset], log_recv.at[offset], chip_at(offset))

    def count_copy(phase, k, device):
        return remote(
            count_out.at[phase], count_in.at[phase, k], count_send.at[phase, k], count_recv.at[phase, k], device
        )

    def grad_copies(which, head):
        out = (dk_ref, dv_ref)[which]
        columns = pl.ds(head * HEAD_SIZE, HEAD_SIZE)
        target = pl.ds(pl.multiple_of(core * HALF + head * HEAD_SIZE, HEAD_SIZE), HEAD_SIZE)
        return [
            pltpu.make_async_copy(
                grads.at[which, my_keys, columns], out.at[:, target], out_local.at[which, head]
            ),
            remote(
                grads.at[which, their_keys, columns],
                out.at[:, target],
                out_send.at[which, head],
                out_recv.at[which, head],
                sibling,
            ),
        ]

    for copy in kv_own:
        copy.start()
    barrier = pltpu.get_barrier_semaphore()
    greeted = [sibling, *ahead, *peers_x, *peers_y]
    for device in greeted:
        pl.semaphore_signal(barrier, inc=1, device_id=device, device_id_type=MESH)

    mask_row = mask_ref[...]
    eye = lax.broadcasted_iota(jnp.int32, (rows, rows), 0) == lax.broadcasted_iota(jnp.int32, (rows, rows), 1)
    mask_column = jnp.sum(jnp.where(eye, mask_row, 0), axis=1, keepdims=True).astype(jnp.float32)
    count_out[2] = jnp.full((8, LANES), jnp.sum(mask_row).astype(jnp.float32))
    stage_out[0] = q_ref[:, theirs].astype(jnp.float32)
    pl.semaphore_wait(barrier, len(greeted))
    staged[0].start()
    stage_out[1] = g_ref[:, theirs].astype(jnp.float32) * mask_column
    staged[1].start()
    stage_out[2] = a_ref[:, theirs].astype(jnp.float32)
    staged[2].start()
    count_swap.start()
    for copy in kv_sent:
        copy.start()

    def both(own, other):
        return jnp.concatenate([jnp.where(core == 0, own, other), jnp.where(core == 0, other, own)], axis=0)

    staged[0].wait_recv()
    qb[0:block, :] = both(q_ref[:, mine].astype(jnp.float32), stage_in[0]).astype(jnp.bfloat16)
    for chunk in range(CHUNKS):
        for way in range(2):
            if chunk in chunks_of_hop(way, 0, slots - 1):
                gathered(0, way, 0, chunk).start()
    staged[1].wait_recv()
    masked = both(g_ref[:, mine].astype(jnp.float32) * mask_column, stage_in[1])
    mb[0:block, :] = masked.astype(jnp.bfloat16)

    staged[2].wait_recv()
    product = masked * both(a_ref[:, mine].astype(jnp.float32), stage_in[2])
    product = jnp.concatenate([product, jnp.zeros((LANES - block, HALF), jnp.float32)], axis=0)
    high = product.astype(jnp.bfloat16)
    low = (product - high.astype(jnp.float32)).astype(jnp.bfloat16)
    head_of = lax.broadcasted_iota(jnp.int32, (8, HALF), 1) // HEAD_SIZE
    picks = (head_of == lax.broadcasted_iota(jnp.int32, (8, HALF), 0) - HALF_HEADS).astype(jnp.bfloat16)
    delta = (nt(picks, high) + nt(picks, low)).astype(jnp.bfloat16).astype(jnp.float32)

    for slot in range(slots):
        for buf in (qb, mb):
            buf[slot * LANES + 2 * block : (slot + 1) * LANES, :] = jnp.zeros(
                (LANES - 2 * block, HALF), jnp.bfloat16
            )

    ends = [in_len[0]]
    row_ends = [out_len[0]]
    for d in range(1, 3):
        ends.append(ends[-1] + in_len[d])
        row_ends.append(row_ends[-1] + out_len[d])
    key_at = z * keys_chip + lax.broadcasted_iota(jnp.int32, (keys_chip, LANES), 0)
    kdoc[...] = sum((key_at >= end).astype(jnp.int32) for end in ends)
    lane = lax.broadcasted_iota(jnp.int32, (1, LANES), 1)

    count_swap.wait_recv()
    chip_count = count_out[2] + count_in[2, 0]

    for copy in (kv_own[0], kv_own[1]):
        copy.wait()
    kv_sent[0].wait_recv()

    def score_slot(slot):
        left = (z - slot + chips) % chips
        right = (z + (slot if slot else slots)) % chips
        at = jnp.where(lane < block, left * block + lane, right * block + lane - block)
        doc = sum((at >= end).astype(jnp.int32) for end in row_ends)
        doc = jnp.where(lane < 2 * block, doc, -1)
        for head in range(HALF_HEADS):
            columns = slice(head * HEAD_SIZE, (head + 1) * HEAD_SIZE)
            s = nt(kx[:, columns], qb[slot * LANES : (slot + 1) * LANES, columns]) * HEAD_SIZE ** (-0.5)
            s = jnp.where(kdoc[...] == doc, s, NEVER)
            scores[slot, head] = s
            top = jnp.max(s, axis=0, keepdims=True)
            tile_out[slot, head : head + 1] = top + jnp.log(jnp.sum(jnp.exp(s - top), axis=0, keepdims=True))
        tile_out[slot, HALF_HEADS:] = chip_count[HALF_HEADS:]
        for copy in tile_copies(slot):
            copy.start()

    def combine_logs():
        for slot in range(slots):
            for copy in tile_copies(slot):
                copy.wait_recv()
        tiles = [tile_out[0]] + [tile_in[i] for i in range(1, slots)]
        tiles += [pltpu.roll(tile_in[i], LANES - block, 1) for i in range(slots, chips)]
        top = functools.reduce(jnp.maximum, tiles)
        total = top + jnp.log(sum(jnp.exp(tile - top) for tile in tiles))
        upper = lax.broadcasted_iota(jnp.int32, (8, LANES), 0) < HALF_HEADS
        log_out[...] = jnp.where(upper, total, delta)
        for offset in range(1, chips):
            log_copy(offset).start()
        group_count = sum(tile[HALF_HEADS : HALF_HEADS + 1, 0:1] for tile in tiles)
        count_out[0] = jnp.broadcast_to(group_count, (8, LANES))
        for k, device in enumerate(peers_x):
            count_copy(0, k, device).start()

    def gather_logs():
        for offset in range(1, chips):
            log_copy(offset).wait_recv()
        for slot in range(slots):
            own = log_out[...] if slot == 0 else log_in[slot]
            far = log_in[chips - slot if slot else slots]
            info = jnp.where(lane < block, own, pltpu.roll(far, block, 1))
            row_info[slot] = jnp.where(lane < 2 * block, info, 0.0)
        total = count_out[0]
        for k, device in enumerate(peers_x):
            count_copy(0, k, device).wait_recv()
            total = total + count_in[0, k]
        count_out[1] = total
        for k, device in enumerate(peers_y):
            count_copy(1, k, device).start()

    def grad_slot(slot):
        for head in range(HALF_HEADS):
            columns = slice(head * HEAD_SIZE, (head + 1) * HEAD_SIZE)
            here = slice(slot * LANES, (slot + 1) * LANES)
            dprob = nt(vx[:, columns], mb[here, columns])
            p = jnp.exp(scores[slot, head] - row_info[slot, head : head + 1])
            ds = p * (dprob - row_info[slot, HALF_HEADS + head : HALF_HEADS + head + 1])
            ds = ds.astype(jnp.bfloat16)
            probs[head, :, here] = p.astype(jnp.bfloat16)
            dscores[head, :, here] = ds
            dq_part[here, columns] = tn(ds, kx[:, columns])

    for hop in range(slots + LAG):
        if hop < slots:
            forward(0, hop)
        if hop == LAG - 1:
            for chunk in range(CHUNKS):
                for way in range(2):
                    if chunk in chunks_of_hop(way, 0, slots - 1):
                        gathered(1, way, 0, chunk).start()
        if LAG <= hop < slots + LAG - 1:
            forward(1, hop - LAG)
        if hop < slots:
            score_slot((hop + 1) % slots)
        if hop == slots:
            combine_logs()
    kv_sent[1].wait_recv()
    gather_logs()
    forward(1, slots - 1)

    def part_for(way, slot, chunk):
        side = slot * LANES + (0 if way and slot else block)
        return dq_part[side : side + block, chunk * wide : (chunk + 1) * wide]

    grad_slot(0)
    for way in range(2):
        for chunk in chunks_of_hop(way, 0, 0):
            rs_out[way, 0, :, chunk * wide : (chunk + 1) * wide] = part_for(way, 0, chunk).astype(jnp.bfloat16)
            scattered(way, 0, chunk).start()
    for hop in range(slots - 1):
        slot = slots - 1 - hop
        grad_slot(slot)
        for chunk in range(CHUNKS):
            columns = slice(chunk * wide, (chunk + 1) * wide)
            for way in range(2):
                part = part_for(way, slot, chunk)
                if chunk in chunks_of_hop(way, hop, 0):
                    scattered(way, hop, chunk).wait_recv()
                    part = part + rs_in[way, hop, :, columns].astype(jnp.float32)
                rs_out[way, hop + 1, :, columns] = part.astype(jnp.bfloat16)
                scattered(way, hop + 1, chunk).start()

    total = count_out[1]
    for k, device in enumerate(peers_y):
        count_copy(1, k, device).wait_recv()
        total = total + count_in[1, k]
    factor = jnp.float32(dp_x * dp_y * chips * block) / total[0:1, 0:1]
    small_factor = factor * HEAD_SIZE ** (-0.5)

    for head in range(HALF_HEADS):
        columns = slice(head * HEAD_SIZE, (head + 1) * HEAD_SIZE)
        grads[1, :, columns] = (nn(probs[head], mb[:, columns]) * factor).astype(jnp.bfloat16)
        for copy in grad_copies(1, head):
            copy.start()
        grads[0, :, columns] = (nn(dscores[head], qb[:, columns]) * small_factor).astype(jnp.bfloat16)
        for copy in grad_copies(0, head):
            copy.start()

    for chunk in range(CHUNKS):
        columns = slice(chunk * wide, (chunk + 1) * wide)
        total = dq_part[0:block, columns]
        for way in range(2):
            scattered(way, slots - 1, chunk).wait_recv()
            total = total + rs_in[way, slots - 1, :, columns].astype(jnp.float32)
        fin[:, columns] = total * small_factor
    my_rows = pl.ds(pl.multiple_of(core * rows, 8), rows)
    their_rows = pl.ds(pl.multiple_of((1 - core) * rows, 8), rows)
    last = remote(fin.at[their_rows], fin_in, fin_send, fin_recv, sibling)
    last.start()
    dq_ref[:, mine] = fin[my_rows, :].astype(jnp.bfloat16)

    for copy in (*staged, count_swap, *kv_sent):
        copy.wait_send()
    for which in range(2):
        for hop in range(slots):
            for way in range(2):
                for chunk in chunks_of_hop(way, hop, slots - 1):
                    gathered(which, way, hop, chunk).wait_send()
    for hop in range(slots):
        for way in range(2):
            for chunk in chunks_of_hop(way, hop, 0):
                scattered(way, hop, chunk).wait_send()
    for slot in range(slots):
        for copy in tile_copies(slot):
            copy.wait_send()
    for offset in range(1, chips):
        log_copy(offset).wait_send()
    for phase, peers in enumerate((peers_x, peers_y)):
        for k, device in enumerate(peers):
            count_copy(phase, k, device).wait_send()
    for which in range(2):
        for head in range(HALF_HEADS):
            near, far = grad_copies(which, head)
            near.wait()
            far.wait()
    last.wait()
    dq_ref[:, theirs] = fin_in[...].astype(jnp.bfloat16)


def local(dp_count, queries, keys, values, attn_out, out_grad, loss_mask, input_lengths, target_lengths):
    rows, features = queries.shape[1:]
    keys_dev = keys.shape[1]
    chips = lax.axis_size("seq") // 2
    slots = chips // 2
    block = 2 * rows
    dp_x, dp_y = (4, 4) if dp_count == 16 else (1, dp_count)
    bf16, f32 = jnp.bfloat16, jnp.float32
    vmem = pl.BlockSpec(memory_space=pltpu.VMEM)
    smem = pl.BlockSpec(memory_space=pltpu.SMEM)
    anywhere = pl.BlockSpec(memory_space=pl.ANY)
    dma = pltpu.SemaphoreType.DMA
    total = chips * block * chips * 2 * keys_dev // chips * HALF
    dq, dk, dv = pl.pallas_call(
        functools.partial(kernel, dp_x, dp_y, chips),
        out_shape=(
            jax.ShapeDtypeStruct((rows, features), bf16),
            jax.ShapeDtypeStruct((keys_dev, features), bf16),
            jax.ShapeDtypeStruct((keys_dev, features), bf16),
        ),
        in_specs=[smem, smem, vmem, vmem, vmem, vmem, anywhere, anywhere],
        out_specs=(vmem, anywhere, anywhere),
        scratch_shapes=[
            pltpu.VMEM((3, rows, HALF), f32),
            pltpu.VMEM((3, rows, HALF), f32),
            pltpu.VMEM((2 * keys_dev, HALF), bf16),
            pltpu.VMEM((2 * keys_dev, HALF), bf16),
            pltpu.VMEM((slots * LANES, HALF), bf16),
            pltpu.VMEM((slots * LANES, HALF), bf16),
            pltpu.VMEM((2 * keys_dev, LANES), jnp.int32),
            pltpu.VMEM((slots, HALF_HEADS, 2 * keys_dev, LANES), f32),
            pltpu.VMEM((HALF_HEADS, 2 * keys_dev, slots * LANES), bf16),
            pltpu.VMEM((HALF_HEADS, 2 * keys_dev, slots * LANES), bf16),
            pltpu.VMEM((slots * LANES, HALF), f32),
            pltpu.VMEM((2, slots, block, HALF), bf16),
            pltpu.VMEM((2, slots, block, HALF), bf16),
            pltpu.VMEM((2, 2 * keys_dev, HALF), bf16),
            pltpu.VMEM((block, HALF), f32),
            pltpu.VMEM((rows, HALF), f32),
            pltpu.VMEM((slots, 8, LANES), f32),
            pltpu.VMEM((chips, 8, LANES), f32),
            pltpu.VMEM((8, LANES), f32),
            pltpu.VMEM((chips, 8, LANES), f32),
            pltpu.VMEM((slots, 8, LANES), f32),
            pltpu.VMEM((3, 8, LANES), f32),
            pltpu.VMEM((3, 3, 8, LANES), f32),
            dma((2,)),
            dma((2,)),
            dma((2,)),
            dma((4,)),
            dma((4,)),
            dma((2, 2, slots, CHUNKS)),
            dma((2, 2, slots, CHUNKS)),
            dma((2, slots, CHUNKS)),
            dma((2, slots, CHUNKS)),
            dma((chips,)),
            dma((chips,)),
            dma((chips,)),
            dma((chips,)),
            dma((2, 3)),
            dma((2, 3)),
            dma((2, HALF_HEADS)),
            dma((2, HALF_HEADS)),
            dma((2, HALF_HEADS)),
            dma,
            dma,
        ],
        compiler_params=pltpu.CompilerParams(
            collective_id=0, has_side_effects=True, vmem_limit_bytes=56 * 1024 * 1024
        ),
        cost_estimate=pl.CostEstimate(flops=10 * total, bytes_accessed=6 * 1024 * 1024, transcendentals=0),
    )(
        input_lengths[0, 0],
        target_lengths[0, 0],
        queries[0],
        out_grad[0],
        attn_out[0],
        loss_mask,
        keys[0],
        values[0],
    )
    return dq[None], dk[None], dv[None]


def solution(mesh):
    return jax.shard_map(
        functools.partial(local, mesh.shape["dp"]),
        mesh=mesh,
        in_specs=(
            P("dp", "seq", None),
            P("dp", "seq", None),
            P("dp", "seq", None),
            P("dp", "seq", None),
            P("dp", "seq", None),
            P("dp", "seq"),
            P("dp", None, None),
            P("dp", None, None),
        ),
        out_specs=(P("dp", "seq", None), P("dp", "seq", None), P("dp", "seq", None)),
        check_vma=False,
    )
```

time: 1130 us -> 109 us (0.10)
  waiting for transfers between devices: 672 us -> 0 us
  starting transfers between devices: 236 us -> 0 us
  blocking collectives: 144 us -> 0 us
  Pallas kernels: 0 us -> 104 us
  other arithmetic: 34.4 us -> 0 us
  local copies, waits for them, and re-layouts: 26.9 us -> 4.91 us
  matrix products: 18.3 us -> 0 us
    ppermute x30 -> x0, waiting for transfers between devices: 672 us -> none  [swapped(): return lax.ppermute(block, axis, route)]
    ppermute x30 -> x0, starting transfers between devices: 236 us -> none  [swapped(): return lax.ppermute(block, axis, route)]
    psum x1 -> x0, blocking collectives: 144 us -> none  [local(): count = lax.psum(jnp.sum(mask_rows).astype(jnp.float32), ('dp', 'seq'))]
    pallas_call x0 -> x1, Pallas kernels: none -> 104 us  [local(): pl.pallas_call(functools.partial(kernel, dp_x, dp_y, chips), out_shape=(j...]
    select_n x23 -> x0, other arithmetic: 21.1 us -> none  [the longest x18 17.6 us: local(): jnp.where(upper, jnp.concatenate([theirs, own_part], 0), jnp.concatenate(...]
    dot_general x5 -> x0, matrix products: 18.3 us -> none  [the longest x1 6.93 us: tile_grads(): jnp.einsum('rhd,ehd->hre', grad_heads, value_heads, preferred_element_typ...]
  transfers between devices with their start and end apart: 30 -> 0, of which waited for: 16 -> 0; matrix products, arithmetic and copies ran while one was open for 5% -> 0% of each run, Pallas kernels for 0% -> 0%
where the time goes in v1:
time: 109 us
  Pallas kernels  104 us (95%)
  local copies, waits for them, and re-layouts  4.91 us (5%)
    pallas_call x1, Pallas kernels, local(): pl.pallas_call(functools.partial(kernel, dp_x, dp_y, chips), out_shape=(j...  104 us
    unnamed x5, local copies, waits for them, and re-layouts  4.91 us

profile of v1, /device:TPU:1, one launch (start us, length us, event | category | flops | bytes accessed | tf_op | source)
XLA Modules:
  0.0 109.2 jit_solution(16756115291216905974)
XLA Ops:
  0.6 103.6 %shard_map.103 = (bf16[24,2048]{1,0:T(8,128)(2,1)}, bf16[256,2048]{1,0:T(8,128)(2,1)}, bf16[256,2048]{1,0:T(8,128)(2,1)}) custom-call(s32[4]{0:T(128)} %bitcast.18, s32[4]{0:T(128)} %bitcast.19, bf16[24,2048]{1,0:T(8,128)(2,1)} %bitcast.15, bf16[24,2048]{1,0:T(8,128)(2,1)} %bitcast.16, bf16[24,2048]{1,0:T(8,128)(2,1)} %bitcast.17, s32[1,24]{1,0:T(1,128)} %mask_ref.1, ...), custom_call_target="tpu_custom_call" | custom-call | flops 4026531840 | bytes 6291456 | tf_op jit(solution)/shard_map/pallas_call | solution.py:447
  104.3 1.5 %copy.14 = bf16[1,24,2048]{2,1,0:T(8,128)(2,1)} copy(bf16[1,24,2048]{2,1,0:T(8,128)(2,1)} %bitcast.12) | data formatting | bytes 196608
  105.8 0.0 copy-start
  105.8 2.4 %copy.15 = bf16[1,256,2048]{2,1,0:T(8,128)(2,1)} copy(bf16[1,256,2048]{2,1,0:T(8,128)(2,1)} %bitcast.11) | data formatting | bytes 2097152
  108.2 0.0 copy-done
  108.2 1.0 copy.16
Async XLA Ops:
  105.8 2.4 %copy-start = (bf16[256,2048]{1,0:T(8,128)(2,1)S(1)}, bf16[256,2048]{1,0:T(8,128)(2,1)}, u32[]{:S(2)}) copy-start(bf16[256,2048]{1,0:T(8,128)(2,1)} %get-tuple-element.8) | copy-start | bytes 3145732

commit v2 on v1

--- a/solution.py
+++ b/solution.py
@@ -13,7 +13,7 @@
 HALF = HALF_HEADS * HEAD_SIZE
 LANES = 128
 CHUNKS = 2
-LAG = 4
+NEAR = 3
 NEVER = -1e30
 MESH = pl.DeviceIdType.MESH
 
@@ -52,7 +52,8 @@
     qb,
     mb,
     kdoc,
-    scores,
+    near_probs,
+    near_dscores,
     probs,
     dscores,
     dq_part,
@@ -65,7 +66,10 @@
     tile_in,
     log_out,
     log_in,
-    row_info,
+    delta_ring,
+    ell_out,
+    ell_in,
+    weights,
     count_out,
     count_in,
     kv_local,
@@ -81,6 +85,10 @@
     tile_recv,
     log_send,
     log_recv,
+    delta_send,
+    delta_recv,
+    ell_send,
+    ell_recv,
     count_send,
     count_recv,
     out_local,
@@ -149,7 +157,39 @@
             return range(CHUNKS)
         return range(CHUNKS // 2) if way == 0 else range(CHUNKS // 2, CHUNKS)
 
+    def delta_copy(way, hop):
+        return remote(
+            delta_ring.at[way, hop],
+            delta_ring.at[way, hop + 1],
+            delta_send.at[way, hop],
+            delta_recv.at[way, hop],
+            ahead[way],
+        )
+
+    def delta_ways(hop):
+        return range(2) if hop + 1 < slots else range(1)
+
+    leap = slots - 1 - NEAR
+
+    def scatter_target(way, hop):
+        if hop == leap:
+            return chip_at(-(NEAR + 1) if way else NEAR + 1)
+        return ahead[way]
+
+    def ell_copy(way, hop):
+        return remote(
+            ell_out.at[way, hop],
+            ell_in.at[way, hop],
+            ell_send.at[way, hop],
+            ell_recv.at[way, hop],
+            scatter_target(way, hop),
+        )
+
     def forward(which, hop):
+        for way in delta_ways(hop) if which else ():
+            delta_copy(way, hop).wait_recv()
+            if hop + 1 < slots and way in delta_ways(hop + 1):
+                delta_copy(way, hop + 1).start()
         for chunk in range(CHUNKS):
             for way in range(2):
                 if chunk in chunks_of_hop(way, hop, slots - 1):
@@ -164,7 +204,7 @@
             rs_in.at[way, hop, :, columns],
             rs_send.at[way, hop, chunk],
             rs_recv.at[way, hop, chunk],
-            ahead[way],
+            scatter_target(way, hop),
         )
 
     def tile_copies(slot):
@@ -235,11 +275,13 @@
     qb[0:block, :] = both(q_ref[:, mine].astype(jnp.float32), stage_in[0]).astype(jnp.bfloat16)
     for chunk in range(CHUNKS):
         for way in range(2):
-            if chunk in chunks_of_hop(way, 0, slots - 1):
-                gathered(0, way, 0, chunk).start()
+            gathered(0, way, 0, chunk).start()
     staged[1].wait_recv()
     masked = both(g_ref[:, mine].astype(jnp.float32) * mask_column, stage_in[1])
     mb[0:block, :] = masked.astype(jnp.bfloat16)
+    for chunk in range(CHUNKS):
+        for way in range(2):
+            gathered(1, way, 0, chunk).start()
 
     staged[2].wait_recv()
     product = masked * both(a_ref[:, mine].astype(jnp.float32), stage_in[2])
@@ -247,8 +289,11 @@
     high = product.astype(jnp.bfloat16)
     low = (product - high.astype(jnp.float32)).astype(jnp.bfloat16)
     head_of = lax.broadcasted_iota(jnp.int32, (8, HALF), 1) // HEAD_SIZE
-    picks = (head_of == lax.broadcasted_iota(jnp.int32, (8, HALF), 0) - HALF_HEADS).astype(jnp.bfloat16)
-    delta = (nt(picks, high) + nt(picks, low)).astype(jnp.bfloat16).astype(jnp.float32)
+    picks = (head_of == lax.broadcasted_iota(jnp.int32, (8, HALF), 0)).astype(jnp.bfloat16)
+    delta = (nt(picks, high) + nt(picks, low)).astype(jnp.bfloat16).astype(jnp.float32)[:HALF_HEADS]
+    for way in range(2):
+        delta_ring[way, 0] = delta
+        delta_copy(way, 0).start()
 
     for slot in range(slots):
         for buf in (qb, mb):
@@ -264,13 +309,10 @@
     key_at = z * keys_chip + lax.broadcasted_iota(jnp.int32, (keys_chip, LANES), 0)
     kdoc[...] = sum((key_at >= end).astype(jnp.int32) for end in ends)
     lane = lax.broadcasted_iota(jnp.int32, (1, LANES), 1)
+    opening = lax.broadcasted_iota(jnp.int32, (HALF_HEADS, LANES), 0) < HALF_HEADS // 2
 
     count_swap.wait_recv()
     chip_count = count_out[2] + count_in[2, 0]
-
-    for copy in (kv_own[0], kv_own[1]):
-        copy.wait()
-    kv_sent[0].wait_recv()
 
     def score_slot(slot):
         left = (z - slot + chips) % chips
@@ -282,10 +324,12 @@
             columns = slice(head * HEAD_SIZE, (head + 1) * HEAD_SIZE)
             s = nt(kx[:, columns], qb[slot * LANES : (slot + 1) * LANES, columns]) * HEAD_SIZE ** (-0.5)
             s = jnp.where(kdoc[...] == doc, s, NEVER)
-            scores[slot, head] = s
             top = jnp.max(s, axis=0, keepdims=True)
-            tile_out[slot, head : head + 1] = top + jnp.log(jnp.sum(jnp.exp(s - top), axis=0, keepdims=True))
-        tile_out[slot, HALF_HEADS:] = chip_count[HALF_HEADS:]
+            e = jnp.exp(s - top)
+            total = jnp.sum(e, axis=0, keepdims=True)
+            near_probs[slot, head] = e * (1.0 / total)
+            ell = top + jnp.log(total)
+            tile_out[slot, head : head + 1] = jnp.where(lane < 2 * block, ell, chip_count[0:1])
         for copy in tile_copies(slot):
             copy.start()
 
@@ -296,12 +340,11 @@
         tiles = [tile_out[0]] + [tile_in[i] for i in range(1, slots)]
         tiles += [pltpu.roll(tile_in[i], LANES - block, 1) for i in range(slots, chips)]
         top = functools.reduce(jnp.maximum, tiles)
-        total = top + jnp.log(sum(jnp.exp(tile - top) for tile in tiles))
-        upper = lax.broadcasted_iota(jnp.int32, (8, LANES), 0) < HALF_HEADS
-        log_out[...] = jnp.where(upper, total, delta)
+        log_out[...] = top + jnp.log(sum(jnp.exp(tile - top) for tile in tiles))
         for offset in range(1, chips):
             log_copy(offset).start()
-        group_count = sum(tile[HALF_HEADS : HALF_HEADS + 1, 0:1] for tile in tiles)
+        counts = [tile_out[0]] + [tile_in[i] for i in range(1, chips)]
+        group_count = sum(tile[0:1, LANES - 1 : LANES] for tile in counts)
         count_out[0] = jnp.broadcast_to(group_count, (8, LANES))
         for k, device in enumerate(peers_x):
             count_copy(0, k, device).start()
@@ -309,11 +352,8 @@
     def gather_logs():
         for offset in range(1, chips):
             log_copy(offset).wait_recv()
-        for slot in range(slots):
-            own = log_out[...] if slot == 0 else log_in[slot]
-            far = log_in[chips - slot if slot else slots]
-            info = jnp.where(lane < block, own, pltpu.roll(far, block, 1))
-            row_info[slot] = jnp.where(lane < 2 * block, info, 0.0)
+
+    def pass_count():
         total = count_out[0]
         for k, device in enumerate(peers_x):
             count_copy(0, k, device).wait_recv()
@@ -322,81 +362,136 @@
         for k, device in enumerate(peers_y):
             count_copy(1, k, device).start()
 
+    def finish_count():
+        total = count_out[1]
+        for k, device in enumerate(peers_y):
+            count_copy(1, k, device).wait_recv()
+            total = total + count_in[1, k]
+        return jnp.float32(dp_x * dp_y * chips * block) / total[0:1, 0:1]
+
     def grad_slot(slot):
+        far = delta_ring[1, slot] if slot else delta_ring[0, slots]
+        deltas = jnp.where(lane < block, delta_ring[0, slot], pltpu.roll(far, block, 1))
+        here = slice(slot * LANES, (slot + 1) * LANES)
         for head in range(HALF_HEADS):
             columns = slice(head * HEAD_SIZE, (head + 1) * HEAD_SIZE)
+            dprob = nt(vx[:, columns], mb[here, columns])
+            ds = near_probs[slot, head] * (dprob - deltas[head : head + 1])
+            near_dscores[slot, head] = ds
+            dq_part[here, columns] = tn(ds.astype(jnp.bfloat16), kx[:, columns])
+
+    def grad_head(head, factor):
+        columns = slice(head * HEAD_SIZE, (head + 1) * HEAD_SIZE)
+        for slot in range(slots):
             here = slice(slot * LANES, (slot + 1) * LANES)
-            dprob = nt(vx[:, columns], mb[here, columns])
-            p = jnp.exp(scores[slot, head] - row_info[slot, head : head + 1])
-            ds = p * (dprob - row_info[slot, HALF_HEADS + head : HALF_HEADS + head + 1])
-            ds = ds.astype(jnp.bfloat16)
-            probs[head, :, here] = p.astype(jnp.bfloat16)
-            dscores[head, :, here] = ds
-            dq_part[here, columns] = tn(ds, kx[:, columns])
-
-    for hop in range(slots + LAG):
-        if hop < slots:
-            forward(0, hop)
-        if hop == LAG - 1:
-            for chunk in range(CHUNKS):
-                for way in range(2):
-                    if chunk in chunks_of_hop(way, 0, slots - 1):
-                        gathered(1, way, 0, chunk).start()
-        if LAG <= hop < slots + LAG - 1:
-            forward(1, hop - LAG)
-        if hop < slots:
-            score_slot((hop + 1) % slots)
-        if hop == slots:
-            combine_logs()
-    kv_sent[1].wait_recv()
-    gather_logs()
-    forward(1, slots - 1)
-
-    def part_for(way, slot, chunk):
+            own = log_out[...] if slot == 0 else log_in[slot]
+            far = pltpu.roll(log_in[chips - slot if slot else slots], block, 1)
+            full = jnp.where(lane < block, own, far)[head : head + 1]
+            scale = jnp.where(lane < 2 * block, jnp.exp(tile_out[slot, head : head + 1] - full), 0.0)
+            probs[:, here] = (near_probs[slot, head] * scale).astype(jnp.bfloat16)
+            dscores[:, here] = (near_dscores[slot, head] * scale).astype(jnp.bfloat16)
+        grads[1, :, columns] = (nn(probs[...], mb[:, columns]) * factor).astype(jnp.bfloat16)
+        for copy in grad_copies(1, head):
+            copy.start()
+        small_factor = factor * HEAD_SIZE ** (-0.5)
+        grads[0, :, columns] = (nn(dscores[...], qb[:, columns]) * small_factor).astype(jnp.bfloat16)
+        for copy in grad_copies(0, head):
+            copy.start()
+
+    for hop in range(slots):
+        slot = (hop + 1) % slots
+        forward(0, hop)
+        if hop == 0:
+            kv_own[0].wait()
+            kv_sent[0].wait_recv()
+        score_slot(slot)
+        forward(1, hop)
+        if hop == 0:
+            kv_own[1].wait()
+            kv_sent[1].wait_recv()
+        grad_slot(slot)
+    ell_out[0, 0] = jnp.where(opening, tile_out[0], NEVER)
+    ell_out[1, 0] = jnp.where(opening, NEVER, pltpu.roll(tile_out[0], LANES - block, 1))
+    for way in range(2):
+        ell_copy(way, 0).start()
+
+    def part_for(way, slot, columns):
         side = slot * LANES + (0 if way and slot else block)
-        return dq_part[side : side + block, chunk * wide : (chunk + 1) * wide]
-
-    grad_slot(0)
+        return dq_part[side : side + block, columns]
+
+    def chunk_columns(chunk):
+        return slice(chunk * wide, (chunk + 1) * wide)
+
     for way in range(2):
         for chunk in chunks_of_hop(way, 0, 0):
-            rs_out[way, 0, :, chunk * wide : (chunk + 1) * wide] = part_for(way, 0, chunk).astype(jnp.bfloat16)
+            columns = chunk_columns(chunk)
+            rs_out[way, 0, :, columns] = part_for(way, 0, columns).astype(jnp.bfloat16)
             scattered(way, 0, chunk).start()
-    for hop in range(slots - 1):
+
+    def scatter_step(hop):
         slot = slots - 1 - hop
-        grad_slot(slot)
+        here = tile_out[slot]
+        if hop == leap:
+            after = here
+        else:
+            for way in range(2):
+                ell_copy(way, hop).wait_recv()
+            before = jnp.where(lane < block, ell_in[1, hop], ell_in[0, hop])
+            top = jnp.maximum(before, here)
+            after = top + jnp.log(jnp.exp(before - top) + jnp.exp(here - top))
+            weights[...] = jnp.concatenate([jnp.exp(before - after), jnp.exp(here - after)], axis=0).T
+        for way in range(2):
+            ell_out[way, hop + 1] = after
+            ell_copy(way, hop + 1).start()
         for chunk in range(CHUNKS):
-            columns = slice(chunk * wide, (chunk + 1) * wide)
             for way in range(2):
-                part = part_for(way, slot, chunk)
-                if chunk in chunks_of_hop(way, hop, 0):
+                arrives = hop != leap and chunk in chunks_of_hop(way, hop, 0)
+                if arrives:
                     scattered(way, hop, chunk).wait_recv()
-                    part = part + rs_in[way, hop, :, columns].astype(jnp.float32)
-                rs_out[way, hop + 1, :, columns] = part.astype(jnp.bfloat16)
+                side = slice(0, block) if way else slice(block, 2 * block)
+                for head in range(chunk * wide // HEAD_SIZE, (chunk + 1) * wide // HEAD_SIZE):
+                    columns = slice(head * HEAD_SIZE, (head + 1) * HEAD_SIZE)
+                    part = part_for(way, slot, columns)
+                    if hop != leap:
+                        part *= weights[side, HALF_HEADS + head : HALF_HEADS + head + 1]
+                    if arrives:
+                        part += rs_in[way, hop, :, columns].astype(jnp.float32) * weights[side, head : head + 1]
+                    rs_out[way, hop + 1, :, columns] = part.astype(jnp.bfloat16)
                 scattered(way, hop + 1, chunk).start()
 
-    total = count_out[1]
-    for k, device in enumerate(peers_y):
-        count_copy(1, k, device).wait_recv()
-        total = total + count_in[1, k]
-    factor = jnp.float32(dp_x * dp_y * chips * block) / total[0:1, 0:1]
+    scatter_step(leap)
+    for step in range(leap):
+        scatter_step(step)
+        if leap + 1 + step < slots - 1:
+            scatter_step(leap + 1 + step)
+        if step == min(1, leap - 1):
+            combine_logs()
+        if step == min(2, leap - 1):
+            pass_count()
+    gather_logs()
+    factor = finish_count()
+    for head in range(HALF_HEADS):
+        grad_head(head, factor)
+
+    for way in range(2):
+        for hop in (leap, slots - 1):
+            ell_copy(way, hop).wait_recv()
+    sums = [(way, hop) for hop in (slots - 1, leap) for way in range(2)]
+    tiles = [ell_in[way, hop] if way else pltpu.roll(ell_in[way, hop], LANES - block, 1) for way, hop in sums]
+    scales = [jnp.exp(jnp.minimum(tile - log_out[...], 0.0)) for tile in (*tiles, tile_out[0], tile_out[0])]
+    columns_of = [jnp.concatenate(scales[i : i + 2], axis=0).T for i in range(0, 6, 2)]
     small_factor = factor * HEAD_SIZE ** (-0.5)
-
-    for head in range(HALF_HEADS):
-        columns = slice(head * HEAD_SIZE, (head + 1) * HEAD_SIZE)
-        grads[1, :, columns] = (nn(probs[head], mb[:, columns]) * factor).astype(jnp.bfloat16)
-        for copy in grad_copies(1, head):
-            copy.start()
-        grads[0, :, columns] = (nn(dscores[head], qb[:, columns]) * small_factor).astype(jnp.bfloat16)
-        for copy in grad_copies(0, head):
-            copy.start()
-
     for chunk in range(CHUNKS):
-        columns = slice(chunk * wide, (chunk + 1) * wide)
-        total = dq_part[0:block, columns]
-        for way in range(2):
-            scattered(way, slots - 1, chunk).wait_recv()
-            total = total + rs_in[way, slots - 1, :, columns].astype(jnp.float32)
-        fin[:, columns] = total * small_factor
+        for way, hop in sums:
+            scattered(way, hop, chunk).wait_recv()
+        for head in range(chunk * wide // HEAD_SIZE, (chunk + 1) * wide // HEAD_SIZE):
+            columns = slice(head * HEAD_SIZE, (head + 1) * HEAD_SIZE)
+            total = dq_part[0:block, columns] * columns_of[2][:block, head : head + 1]
+            for i, (way, hop) in enumerate(sums):
+                part = rs_in[way, hop, :, columns].astype(jnp.float32)
+                at = i % 2 * HALF_HEADS + head
+                total += part * columns_of[i // 2][:block, at : at + 1]
+            fin[:, columns] = total * small_factor
     my_rows = pl.ds(pl.multiple_of(core * rows, 8), rows)
     their_rows = pl.ds(pl.multiple_of((1 - core) * rows, 8), rows)
     last = remote(fin.at[their_rows], fin_in, fin_send, fin_recv, sibling)
@@ -414,6 +509,11 @@
         for way in range(2):
             for chunk in chunks_of_hop(way, hop, 0):
                 scattered(way, hop, chunk).wait_send()
+    for hop in range(slots):
+        for way in range(2):
+            ell_copy(way, hop).wait_send()
+        for way in delta_ways(hop):
+            delta_copy(way, hop).wait_send()
     for slot in range(slots):
         for copy in tile_copies(slot):
             copy.wait_send()
@@ -429,6 +529,31 @@
             far.wait()
     last.wait()
     dq_ref[:, theirs] = fin_in[...].astype(jnp.bfloat16)
+
+
+def hand_over(*refs):
+    sources, targets, held = refs[:3], refs[3:6], refs[6:9]
+    in_sems, out_sems = refs[9:]
+    pieces = []
+    for source, target, buf in zip(sources, targets, held):
+        parts = 4 if source.shape[0] % 64 == 0 else 1
+        size = source.shape[0] // parts
+        for part in range(parts):
+            rows = pl.ds(part * size, size)
+            i = len(pieces)
+            pieces.append(
+                (
+                    pltpu.make_async_copy(source.at[rows], buf.at[rows], in_sems.at[i]),
+                    pltpu.make_async_copy(buf.at[rows], target.at[rows], out_sems.at[i]),
+                )
+            )
+    for fetch, _ in pieces:
+        fetch.start()
+    for fetch, store in pieces:
+        fetch.wait()
+        store.start()
+    for _, store in pieces:
+        store.wait()
 
 
 def local(dp_count, queries, keys, values, attn_out, out_grad, loss_mask, input_lengths, target_lengths):
@@ -462,19 +587,23 @@
             pltpu.VMEM((slots * LANES, HALF), bf16),
             pltpu.VMEM((2 * keys_dev, LANES), jnp.int32),
             pltpu.VMEM((slots, HALF_HEADS, 2 * keys_dev, LANES), f32),
-            pltpu.VMEM((HALF_HEADS, 2 * keys_dev, slots * LANES), bf16),
-            pltpu.VMEM((HALF_HEADS, 2 * keys_dev, slots * LANES), bf16),
+            pltpu.VMEM((slots, HALF_HEADS, 2 * keys_dev, LANES), f32),
+            pltpu.VMEM((2 * keys_dev, slots * LANES), bf16),
+            pltpu.VMEM((2 * keys_dev, slots * LANES), bf16),
             pltpu.VMEM((slots * LANES, HALF), f32),
             pltpu.VMEM((2, slots, block, HALF), bf16),
             pltpu.VMEM((2, slots, block, HALF), bf16),
             pltpu.VMEM((2, 2 * keys_dev, HALF), bf16),
             pltpu.VMEM((block, HALF), f32),
             pltpu.VMEM((rows, HALF), f32),
-            pltpu.VMEM((slots, 8, LANES), f32),
-            pltpu.VMEM((chips, 8, LANES), f32),
-            pltpu.VMEM((8, LANES), f32),
-            pltpu.VMEM((chips, 8, LANES), f32),
-            pltpu.VMEM((slots, 8, LANES), f32),
+            pltpu.VMEM((slots, HALF_HEADS, LANES), f32),
+            pltpu.VMEM((chips, HALF_HEADS, LANES), f32),
+            pltpu.VMEM((HALF_HEADS, LANES), f32),
+            pltpu.VMEM((chips, HALF_HEADS, LANES), f32),
+            pltpu.VMEM((2, slots + 1, HALF_HEADS, LANES), f32),
+            pltpu.VMEM((2, slots, HALF_HEADS, LANES), f32),
+            pltpu.VMEM((2, slots, HALF_HEADS, LANES), f32),
+            pltpu.VMEM((LANES, 2 * HALF_HEADS), f32),
             pltpu.VMEM((3, 8, LANES), f32),
             pltpu.VMEM((3, 3, 8, LANES), f32),
             dma((2,)),
@@ -490,6 +619,10 @@
             dma((chips,)),
             dma((chips,)),
             dma((chips,)),
+            dma((2, slots)),
+            dma((2, slots)),
+            dma((2, slots)),
+            dma((2, slots)),
             dma((2, 3)),
             dma((2, 3)),
             dma((2, HALF_HEADS)),
@@ -512,6 +645,16 @@
         keys[0],
         values[0],
     )
+    results = (dk, dv, dq)
+    dk, dv, dq = pl.pallas_call(
+        hand_over,
+        out_shape=tuple(jax.ShapeDtypeStruct(array.shape, array.dtype) for array in results),
+        in_specs=[anywhere] * 3,
+        out_specs=(anywhere,) * 3,
+        scratch_shapes=[*(pltpu.VMEM(array.shape, array.dtype) for array in results), dma((9,)), dma((9,))],
+        compiler_params=pltpu.CompilerParams(vmem_limit_bytes=56 * 1024 * 1024),
+        cost_estimate=pl.CostEstimate(flops=0, bytes_accessed=5 * 1024 * 1024, transcendentals=0),
+    )(*results)
     return dq[None], dk[None], dv[None]
 
 

time: 109 us -> 90.5 us (0.83)
  Pallas kernels: 104 us -> 89.5 us
  local copies, waits for them, and re-layouts: 4.91 us -> 0 us
    pallas_call x1, Pallas kernels: 104 us -> 87 us  [local(): pl.pallas_call(functools.partial(kernel, dp_x, dp_y, chips), out_shape=(j...]
    unnamed x5 -> x0, local copies, waits for them, and re-layouts: 4.91 us -> none
    pallas_call x0 -> x1, Pallas kernels: none -> 2.44 us  [local(): pl.pallas_call(hand_over, out_shape=tuple((jax.ShapeDtypeStruct(array.sha...]
where the time goes in v2:
time: 90.5 us; the launch traced here: 90.3 us
  Pallas kernels  89.5 us (99%)
    pallas_call x1, Pallas kernels, local(): pl.pallas_call(functools.partial(kernel, dp_x, dp_y, chips), out_shape=(j...  87 us
    pallas_call x1, Pallas kernels, local(): pl.pallas_call(hand_over, out_shape=tuple((jax.ShapeDtypeStruct(array.sha...  2.44 us

profile of v2, /device:TPU:1, one launch (start us, length us, event | category | flops | bytes accessed | tf_op | source)
XLA Modules:
  0.0 90.3 jit_solution(3826205556732046257)
XLA Ops:
  0.6 87.0 %shard_map.103 = (bf16[24,2048]{1,0:T(8,128)(2,1)}, bf16[256,2048]{1,0:T(8,128)(2,1)}, bf16[256,2048]{1,0:T(8,128)(2,1)}) custom-call(s32[4]{0:T(128)} %bitcast.18, s32[4]{0:T(128)} %bitcast.19, bf16[24,2048]{1,0:T(8,128)(2,1)} %bitcast.14, bf16[24,2048]{1,0:T(8,128)(2,1)} %bitcast.15, bf16[24,2048]{1,0:T(8,128)(2,1)} %bitcast.16, s32[1,24]{1,0:T(1,128)} %mask_ref.1, ...), custom_call_target="tpu_custom_call" | custom-call | flops 4026531840 | bytes 6291456 | tf_op jit(solution)/shard_map/pallas_call | solution.py:572
  87.7 2.4 %shard_map.104 = (bf16[256,2048]{1,0:T(8,128)(2,1)}, bf16[256,2048]{1,0:T(8,128)(2,1)}, bf16[24,2048]{1,0:T(8,128)(2,1)}) custom-call(bf16[256,2048]{1,0:T(8,128)(2,1)} %get-tuple-element.9.refs_0_, bf16[256,2048]{1,0:T(8,128)(2,1)} %get-tuple-element.10.refs_1_, bf16[24,2048]{1,0:T(8,128)(2,1)} %get-tuple-element.11.refs_2_), custom_call_target="tpu_custom_call" | custom-call | bytes 5242880 | tf_op jit(solution)/shard_map/pallas_call | solution.py:649

commit v3 on v2

--- a/solution.py
+++ b/solution.py
@@ -265,8 +265,6 @@
     stage_out[2] = a_ref[:, theirs].astype(jnp.float32)
     staged[2].start()
     count_swap.start()
-    for copy in kv_sent:
-        copy.start()
 
     def both(own, other):
         return jnp.concatenate([jnp.where(core == 0, own, other), jnp.where(core == 0, other, own)], axis=0)
@@ -282,6 +280,8 @@
     for chunk in range(CHUNKS):
         for way in range(2):
             gathered(1, way, 0, chunk).start()
+    for copy in kv_sent:
+        copy.start()
 
     staged[2].wait_recv()
     product = masked * both(a_ref[:, mine].astype(jnp.float32), stage_in[2])
@@ -341,7 +341,7 @@
         tiles += [pltpu.roll(tile_in[i], LANES - block, 1) for i in range(slots, chips)]
         top = functools.reduce(jnp.maximum, tiles)
         log_out[...] = top + jnp.log(sum(jnp.exp(tile - top) for tile in tiles))
-        for offset in range(1, chips):
+        for offset in sorted(range(1, chips), key=lambda offset: abs(offset - slots)):
             log_copy(offset).start()
         counts = [tile_out[0]] + [tile_in[i] for i in range(1, chips)]
         group_count = sum(tile[0:1, LANES - 1 : LANES] for tile in counts)
@@ -398,35 +398,12 @@
         for copy in grad_copies(0, head):
             copy.start()
 
-    for hop in range(slots):
-        slot = (hop + 1) % slots
-        forward(0, hop)
-        if hop == 0:
-            kv_own[0].wait()
-            kv_sent[0].wait_recv()
-        score_slot(slot)
-        forward(1, hop)
-        if hop == 0:
-            kv_own[1].wait()
-            kv_sent[1].wait_recv()
-        grad_slot(slot)
-    ell_out[0, 0] = jnp.where(opening, tile_out[0], NEVER)
-    ell_out[1, 0] = jnp.where(opening, NEVER, pltpu.roll(tile_out[0], LANES - block, 1))
-    for way in range(2):
-        ell_copy(way, 0).start()
-
     def part_for(way, slot, columns):
         side = slot * LANES + (0 if way and slot else block)
         return dq_part[side : side + block, columns]
 
     def chunk_columns(chunk):
         return slice(chunk * wide, (chunk + 1) * wide)
-
-    for way in range(2):
-        for chunk in chunks_of_hop(way, 0, 0):
-            columns = chunk_columns(chunk)
-            rs_out[way, 0, :, columns] = part_for(way, 0, columns).astype(jnp.bfloat16)
-            scattered(way, 0, chunk).start()
 
     def scatter_step(hop):
         slot = slots - 1 - hop
@@ -459,13 +436,37 @@
                     rs_out[way, hop + 1, :, columns] = part.astype(jnp.bfloat16)
                 scattered(way, hop + 1, chunk).start()
 
-    scatter_step(leap)
+    for hop in range(slots):
+        slot = (hop + 1) % slots
+        forward(0, hop)
+        if hop == 0:
+            kv_own[0].wait()
+            kv_sent[0].wait_recv()
+        score_slot(slot)
+        forward(1, hop)
+        if hop == 0:
+            kv_own[1].wait()
+            kv_sent[1].wait_recv()
+        grad_slot(slot)
+        if hop == slots - 2:
+            scatter_step(leap)
+    ell_out[0, 0] = jnp.where(opening, tile_out[0], NEVER)
+    ell_out[1, 0] = jnp.where(opening, NEVER, pltpu.roll(tile_out[0], LANES - block, 1))
+    for way in range(2):
+        ell_copy(way, 0).start()
+
+    for way in range(2):
+        for chunk in chunks_of_hop(way, 0, 0):
+            columns = chunk_columns(chunk)
+            rs_out[way, 0, :, columns] = part_for(way, 0, columns).astype(jnp.bfloat16)
+            scattered(way, 0, chunk).start()
+
     for step in range(leap):
         scatter_step(step)
+        if step == min(1, leap - 1):
+            combine_logs()
         if leap + 1 + step < slots - 1:
             scatter_step(leap + 1 + step)
-        if step == min(1, leap - 1):
-            combine_logs()
         if step == min(2, leap - 1):
             pass_count()
     gather_logs()
@@ -496,7 +497,7 @@
     their_rows = pl.ds(pl.multiple_of((1 - core) * rows, 8), rows)
     last = remote(fin.at[their_rows], fin_in, fin_send, fin_recv, sibling)
     last.start()
-    dq_ref[:, mine] = fin[my_rows, :].astype(jnp.bfloat16)
+    dq_ref[:, mine] = fin[my_rows, :]
 
     for copy in (*staged, count_swap, *kv_sent):
         copy.wait_send()
@@ -528,12 +529,13 @@
             near.wait()
             far.wait()
     last.wait()
-    dq_ref[:, theirs] = fin_in[...].astype(jnp.bfloat16)
+    dq_ref[:, theirs] = fin_in[...]
 
 
 def hand_over(*refs):
-    sources, targets, held = refs[:3], refs[3:6], refs[6:9]
-    in_sems, out_sems = refs[9:]
+    sources, targets, held = refs[:2], refs[3:5], refs[6:8]
+    dq_in, dq_out, dq_held = refs[2], refs[5], refs[8]
+    in_sems, out_sems, dq_sem = refs[9:]
     pieces = []
     for source, target, buf in zip(sources, targets, held):
         parts = 4 if source.shape[0] % 64 == 0 else 1
@@ -547,11 +549,15 @@
                     pltpu.make_async_copy(buf.at[rows], target.at[rows], out_sems.at[i]),
                 )
             )
+    dq_fetch = pltpu.make_async_copy(dq_in, dq_held, dq_sem)
     for fetch, _ in pieces:
         fetch.start()
+    dq_fetch.start()
     for fetch, store in pieces:
         fetch.wait()
         store.start()
+    dq_fetch.wait()
+    dq_out[...] = dq_held[...].astype(dq_out.dtype)
     for _, store in pieces:
         store.wait()
 
@@ -572,7 +578,7 @@
     dq, dk, dv = pl.pallas_call(
         functools.partial(kernel, dp_x, dp_y, chips),
         out_shape=(
-            jax.ShapeDtypeStruct((rows, features), bf16),
+            jax.ShapeDtypeStruct((rows, features), f32),
             jax.ShapeDtypeStruct((keys_dev, features), bf16),
             jax.ShapeDtypeStruct((keys_dev, features), bf16),
         ),
@@ -648,10 +654,10 @@
     results = (dk, dv, dq)
     dk, dv, dq = pl.pallas_call(
         hand_over,
-        out_shape=tuple(jax.ShapeDtypeStruct(array.shape, array.dtype) for array in results),
+        out_shape=tuple(jax.ShapeDtypeStruct(array.shape, bf16) for array in results),
         in_specs=[anywhere] * 3,
-        out_specs=(anywhere,) * 3,
-        scratch_shapes=[*(pltpu.VMEM(array.shape, array.dtype) for array in results), dma((9,)), dma((9,))],
+        out_specs=(anywhere, anywhere, vmem),
+        scratch_shapes=[*(pltpu.VMEM(array.shape, array.dtype) for array in results), dma((8,)), dma((8,)), dma],
         compiler_params=pltpu.CompilerParams(vmem_limit_bytes=56 * 1024 * 1024),
         cost_estimate=pl.CostEstimate(flops=0, bytes_accessed=5 * 1024 * 1024, transcendentals=0),
     )(*results)

time: 90.5 us -> 90.4 us (level)
  no operation moved by 1% of the time
where the time goes in v3:
time: 90.4 us; the launch traced here: 90.2 us
  Pallas kernels  89.4 us (99%)
    pallas_call x1, Pallas kernels, local(): pl.pallas_call(functools.partial(kernel, dp_x, dp_y, chips), out_shape=(j...  86.3 us
    pallas_call x1, Pallas kernels, local(): pl.pallas_call(hand_over, out_shape=tuple((jax.ShapeDtypeStruct(array.sha...  3.04 us

profile of v3, /device:TPU:1, one launch (start us, length us, event | category | flops | bytes accessed | tf_op | source)
XLA Modules:
  0.0 90.2 jit_solution(12980908995575392771)
XLA Ops:
  0.6 86.3 %shard_map.103 = (f32[24,2048]{1,0:T(8,128)}, bf16[256,2048]{1,0:T(8,128)(2,1)}, bf16[256,2048]{1,0:T(8,128)(2,1)}) custom-call(s32[4]{0:T(128)} %bitcast.18, s32[4]{0:T(128)} %bitcast.19, bf16[24,2048]{1,0:T(8,128)(2,1)} %bitcast.14, bf16[24,2048]{1,0:T(8,128)(2,1)} %bitcast.15, bf16[24,2048]{1,0:T(8,128)(2,1)} %bitcast.16, s32[1,24]{1,0:T(1,128)} %mask_ref.1, ...), custom_call_target="tpu_custom_call" | custom-call | flops 4026531840 | bytes 6291456 | tf_op jit(solution)/shard_map/pallas_call | solution.py:578
  87.0 3.0 %shard_map.104 = (bf16[256,2048]{1,0:T(8,128)(2,1)}, bf16[256,2048]{1,0:T(8,128)(2,1)}, bf16[24,2048]{1,0:T(8,128)(2,1)}) custom-call(bf16[256,2048]{1,0:T(8,128)(2,1)} %get-tuple-element.9.refs_0_, bf16[256,2048]{1,0:T(8,128)(2,1)} %get-tuple-element.10.refs_1_, f32[24,2048]{1,0:T(8,128)} %get-tuple-element.11.refs_2_), custom_call_target="tpu_custom_call" | custom-call | bytes 5242880 | tf_op jit(solution)/shard_map/pallas_call | solution.py:655
